TPU v7x, 32 devices: a whole 2x2x4 slice. The times are simulated.
32 devices in a mesh: orb: 4 (over z), pair: 8 (over y, x, core).
Axes of the slice: x: 2, y: 2, z: 4, core: 2. Of those that a mesh axis runs over, the one named last changes fastest.
Arguments:
- blocks: bfloat16 [128, 1024, 320], P(('orb', 'pair')), may hold values from -1.1953125 to 1.1953125
- aux_domain: int32 [128, 1024], replicated, may hold values from 0 to 2047, as said below
- pao_domain: int32 [128, 320], replicated, may hold values from -1 to 639, as said below
- pao_gap: float32 [128, 320], replicated, may hold values from 1 to 4
- amplitudes: bfloat16 [256, 320, 320], P(('orb', 'pair')), may hold values from -3 to 3
- pair_partner: int32 [256], replicated, may hold values from 0 to 127, as said below
- coupling_list: int32 [256, 4], P(('orb', 'pair')), may hold values from 0 to 255, as said below
- coupling_coef: float32 [256, 4], P(('orb', 'pair')), may hold values from -0.6 to 0.6
Outputs:
- new_amplitudes: bfloat16 [256, 320, 320], P(('orb', 'pair'))
- pair_energy: float32 [256], P(('orb', 'pair'))
- densities: float32 [128, 320, 320], P(('orb', 'pair'))
Inputs may be any that keep to these rules, and one draw needn't show every extreme that they name: `aux_domain`: each row holds 1024 distinct auxiliary function ids. `pao_domain`: each row holds distinct PAO ids in its leading slots and -1 in the rest; at least 160 ids a row. With d = p // 8, pair_partner[p] lies in [(d - 1) * 4, (d + 2) * 4). `coupling_list`: row p lists pair ids q with 0 < |q - p| <= 8.
All inputs are finite; a program needn't handle non-finite values.
Results may differ from a plain program's by a relative error of at most 0.003.
Values may be sent and summed in bfloat16 or wider, within the bound.
No kernel may reach another device: no remote copies, remote signals or barrier semaphores. Data moves between devices by JAX's collectives and lax.ppermute only.
A program may use at most 128 MiB of HBM per device.

v0:
```python
import functools

import jax
import jax.numpy as jnp
from jax import lax
from jax.experimental import pallas as pl
from jax.experimental.pallas import tpu as pltpu
from jax.sharding import PartitionSpec as P

AXES = ("orb", "pair")
MIB = 1024 * 1024
AUX_IDS = 2048
LOW = 64
HIGH = AUX_IDS // LOW
BASE = 32
LANES = 128
FIRST, WHOLE = 40, 64
NN = (((1,), (0,)), ((), ()))
NT = (((1,), (1,)), ((), ()))
TN = (((0,), (0,)), ((), ()))


def dot(a, b, dims=NN):
    return lax.dot_general(a, b, dims, preferred_element_type=jnp.float32)


def one_where(equal, value=1.0):
    return jnp.where(equal, value, 0.0).astype(jnp.bfloat16)


def iota(shape, dim):
    return lax.broadcasted_iota(jnp.int32, shape, dim)


def live(rows, cols, shape):
    return (iota(shape, 0) < rows) & (iota(shape, 1) < cols)


def kept(amp, rows, cols):
    return jnp.where(live(rows, cols, amp.shape), amp.astype(jnp.float32), 0.0).astype(amp.dtype)


def short_where(equal):
    one = jnp.ones(equal.shape, jnp.bfloat16)
    return jnp.where(equal, one, jnp.zeros_like(one))


def column(row):
    return jnp.broadcast_to(row, (LANES, row.shape[1])).T


def same(col, row):
    parts = []
    for at in range(0, row.shape[1], LANES):
        piece = row[:, at : at + LANES]
        wide = jnp.broadcast_to(piece, (col.shape[0], piece.shape[1]))
        parts.append(short_where(col[:, : piece.shape[1]] == wide))
    return jnp.concatenate(parts, axis=1)


def chunks_of(count):
    return (count + LANES - 1) // LANES


def rows_of(length):
    return (length + 15) // 16 * 16


def swapped(me):
    odd = lax.rem(me, 2)
    return me + 1 - 2 * odd, me - 1 + 2 * odd


class Sizes:
    def __init__(self, blocks, amplitudes, pair_partner):
        self.occ = blocks.shape[0]
        self.aux = blocks.shape[1]
        self.pao = blocks.shape[2]
        self.pairs = amplitudes.shape[0]
        self.npair = pair_partner.shape[0]
        self.nocc = self.npair // self.pairs * self.occ
        self.rows = self.occ * self.pao * (self.aux // LANES)
        self.first = self.rows * FIRST // WHOLE // 16 * 16
        self.room = self.first - self.pao // 2

    def first_orbital(self, pair):
        return pair // self.pairs * self.occ + lax.rem(pair, self.occ)

    def where_partner(self, me, right):
        device = right // self.occ
        sibling, _ = swapped(me)
        kind = jnp.where(device == me, 2, jnp.where(device == sibling, 0, 1))
        return kind * self.occ + lax.rem(right, self.occ), kind


def packing(s):
    whole = s.pao // LANES * LANES
    tail = s.pao - whole
    share = whole // tail
    return whole, tail, share


def slim_kernel(s, amps, out):
    whole, tail, share = packing(s)
    for k in range(s.pairs):
        out[k] = amps[k, :, :whole]
    for g in range(s.pairs // share):
        tails = [amps[g * share + t, :, whole:] for t in range(share)]
        out[s.pairs + g] = jnp.concatenate(tails, axis=1)


def unpack(s, packed, k, out):
    whole, tail, share = packing(s)
    out[:, :whole] = packed[k]
    spot = k % share * tail
    out[:, whole:] = packed[s.pairs + k // share, :, spot : spot + tail]


def bits(values, count, lanes):
    levels = iota((count, lanes), 0).astype(jnp.bfloat16)
    return short_where(levels == jnp.broadcast_to(values.astype(jnp.bfloat16), (count, lanes)))


def places(row, table, k):
    found = dot(table, bits(row // LOW + k * HIGH, table.shape[1], row.shape[1]))
    low = bits(lax.rem(row, LOW), LOW, row.shape[1]).astype(jnp.float32)
    return jnp.sum((found[:LOW] * BASE + found[LOW:]) * low, axis=0, keepdims=True)


def picker(place, chunk):
    wide = 2 * LANES
    middle = chunk * wide + LANES + 1
    spot = (place - jnp.asarray(middle).astype(jnp.float32)).astype(jnp.bfloat16)
    levels = (iota((wide, place.shape[1]), 0) - LANES).astype(jnp.bfloat16)
    return short_where(levels == jnp.broadcast_to(spot, levels.shape))


def chunkwise(s, count, act):
    for c in range(s.aux // (2 * LANES)):
        pl.when(count > c * 2 * LANES)(functools.partial(act, c))


def split_place(place, row):
    part = jnp.where(row < LOW, place // BASE, lax.rem(place, BASE))
    return part.astype(jnp.float32).astype(jnp.bfloat16)


def pack_kernel(
    s, here, partner, lens, aux_rows, blocks, pao_cols, gap_cols, _, to_sibling, to_other, to_other_more, tables, pao_rows, gap_rows, counts, offsets, maps, users, sends, needed, bufs, sems
):
    me = here[0]
    peers = swapped(me)
    pao_rows[...] = pao_cols[...].T
    gap_rows[...] = gap_cols[...].T

    for g, device in enumerate((me,) + peers):
        for k in range(s.occ):
            orbital = jnp.clip(device * s.occ + k, 0, s.nocc - 1)
            row = aux_rows[pl.ds(orbital, 1), :]
            by_high = bits(row // LOW, HIGH, s.aux)
            by_low = bits(lax.rem(row, LOW), LOW, s.aux)
            here_map = dot(jnp.concatenate([by_low, by_low], axis=0), by_high, NT)
            maps[g, :, k * HIGH : (k + 1) * HIGH] = here_map
            users[g * s.occ + k] = jnp.concatenate([here_map] * s.occ, axis=1)
            if g == 0:
                spot = iota((LOW, s.aux), 1) + 1
                parts = jnp.concatenate(
                    [
                        (spot // BASE).astype(jnp.float32).astype(jnp.bfloat16) * by_low,
                        lax.rem(spot, BASE).astype(jnp.float32).astype(jnp.bfloat16) * by_low,
                    ],
                    axis=0,
                )
                tables[2, :, k * HIGH : (k + 1) * HIGH] = dot(parts, by_high, NT).astype(
                    jnp.bfloat16
                )

    wide = s.occ * HIGH
    sub, lane = iota((2 * LOW, 2 * LOW), 0), iota((2 * LOW, 2 * LOW), 1)
    ahead = one_where((lane < LOW) & (lane < lax.rem(sub, LOW)))
    first = one_where(lane < LOW)
    sub, lane = iota((wide, wide), 0), iota((wide, wide), 1)
    above = one_where((sub // HIGH == lane // HIGH) & (sub < lane))
    level = iota((2 * LOW, wide), 0)
    owner = iota((1, wide), 1) // HIGH

    def listing(target, target_device, user, user_device):
        union = jnp.zeros((2 * LOW, wide), jnp.float32)
        for q in range(s.occ):
            uses = jnp.zeros((1, wide), jnp.float32)
            for pair in range(q, s.pairs, s.occ):
                pair += user_device * s.pairs
                inside = (pair >= 0) & (pair < s.npair)
                k = partner[jnp.clip(pair, 0, s.npair - 1)] - target_device * s.occ
                uses += jnp.where((owner == k) & inside, 1.0, 0.0)
            union += uses * users[user * s.occ + q]
        taken = (union > 0.0) & (maps[target] > 0.0)
        flags = one_where(taken)
        total = dot(first, flags)
        place = dot(ahead, flags) + dot(total.astype(jnp.bfloat16), above) + 1.0
        place = jnp.where(taken, place, 0.0).astype(jnp.int32)
        found = [
            jnp.sum(jnp.where(owner == k, total[:1], 0.0)).astype(jnp.int32) for k in range(s.occ)
        ]
        return split_place(place, level), found

    copies = {
        0: [pltpu.make_async_copy(bufs.at[0, pl.ds(0, s.rows)], to_sibling, sems.at[0])],
        1: [
            pltpu.make_async_copy(bufs.at[1, pl.ds(0, s.first)], to_other, sems.at[1]),
            pltpu.make_async_copy(
                bufs.at[1, pl.ds(s.first, s.rows - s.first)], to_other_more, sems.at[2]
            ),
        ],
    }
    for r in (1, 0):
        sends[r], found = listing(0, me, 1 + r, peers[r])
        for k, count in enumerate(found):
            needed[k] = count

        def send(k, at, r=r):
            count = needed[k]
            step = rows_of(lens[me * s.occ + k])

            @pl.when(count > 0)
            def _():
                place = places(aux_rows[pl.ds(me * s.occ + k, 1), :], sends[r], k)

                def some(c):
                    got = dot(blocks[k], picker(place, c), NT).astype(jnp.bfloat16)
                    spot = pl.multiple_of(at + 2 * c * step, 16)
                    bufs[r, pl.ds(spot, s.pao), :] = got[:, :LANES]

                    @pl.when((2 * c + 1) * LANES < count)
                    def _():
                        bufs[r, pl.ds(pl.multiple_of(spot + step, 16), s.pao), :] = got[:, LANES:]

                chunkwise(s, count, some)

            return at + chunks_of(count) * step

        lax.fori_loop(0, s.occ, send, jnp.int32(0))
        for copy in copies[r]:
            copy.start()

    for r in range(2):
        tables[r], found = listing(1 + r, peers[r], 0, me)
        at = jnp.int32(0)
        for k, count in enumerate(found):
            orbital = jnp.clip(peers[r] * s.occ + k, 0, s.nocc - 1)
            counts[r * s.occ + k] = count
            offsets[r * s.occ + k] = at
            at += chunks_of(count) * rows_of(lens[orbital])
    for k in range(s.occ):
        counts[2 * s.occ + k] = jnp.int32(s.aux)
        offsets[2 * s.occ + k] = jnp.int32(0)

    for copy in copies[1] + copies[0]:
        copy.wait()


def count_kernel(s, partner, lens, aux_rows, _, over):
    devices = s.nocc // s.occ
    full = s.aux // LANES

    def ids(orbital):
        row = aux_rows[pl.ds(orbital, 1), :]
        return dot(bits(row // LOW, HIGH, s.aux), bits(lax.rem(row, LOW), LOW, s.aux), NT)

    over[0] = jnp.int32(0)

    def edge(e, _):
        source = e + 1
        user = source + 1 - 2 * lax.rem(e, 2)
        reads = [partner[user * s.pairs + q] - source * s.occ for q in range(s.pairs)]
        bound = jnp.int32(0)
        for k in range(s.occ):
            used = functools.reduce(jnp.logical_or, [read == k for read in reads])
            bound += jnp.where(used, full * rows_of(lens[source * s.occ + k]), 0)

        @pl.when(bound > s.room)
        def _():
            domains = [ids(user * s.occ + q) for q in range(s.occ)]
            need = jnp.int32(0)
            for k in range(s.occ):
                union = jnp.zeros((HIGH, LOW), jnp.float32)
                for q, domain in enumerate(domains):
                    used = functools.reduce(
                        jnp.logical_or, [read == k for read in reads[q :: s.occ]]
                    )
                    union += jnp.where(used, 1.0, 0.0) * domain
                taken = (union > 0.0) & (ids(source * s.occ + k) > 0.0)
                count = jnp.sum(jnp.where(taken, 1.0, 0.0)).astype(jnp.int32)
                need += chunks_of(count) * rows_of(lens[source * s.occ + k])
            over[0] = jnp.maximum(over[0], (need > s.room).astype(jnp.int32))

        return 0

    lax.fori_loop(0, devices - 2, edge, 0)


def own_kernel(
    s, here, partner, lens, counts, tables, aux_rows, blocks, amps, _, __, aligned, dens, ___, ____
):
    left = pl.program_id(0)
    me = here[0]
    wide = 2 * LANES
    chunks = s.aux // wide
    row = aux_rows[pl.ds(me * s.occ + left, 1), :]
    term = jnp.zeros((s.pao, s.pao), jnp.float32)
    rest = []

    for t in range(s.pairs // s.occ):
        right = partner[me * s.pairs + t * s.occ + left]
        l, kind = s.where_partner(me, right)
        place = places(row, tables[kind], lax.rem(right, s.occ))

        def some(c, t=t, place=place):
            aligned[t, 0, :, c * wide : (c + 1) * wide] = dot(
                blocks[0], picker(place, c), NT
            ).astype(jnp.bfloat16)

        for c in range(chunks - 1):
            some(c)
        rest.append((counts[l] > (chunks - 1) * wide, functools.partial(some, chunks - 1)))
        masked = kept(amps[t, 0], lens[me * s.occ + left], lens[right])
        term += dot(masked, masked, NT)

    dens[0] = term
    for needed, act in rest:
        pl.when(needed)(act)


def column_of(pao_rows, orbital):
    row = pao_rows[pl.ds(orbital, 1), :]
    return column(jnp.where(row < 0, -2, row)).astype(jnp.int16)


def row_of(pao_rows, orbital):
    return pao_rows[pl.ds(orbital, 1), :]


def near_kernel(
    s, ncpl, here, partner, listed, lens, coef, counts, offsets, _, pao_rows, sibling, own, aligned, dens_in, blocks, from_sibling, coupling, exchange, dens, wide, tall, dens_own, near_blocks, halo, sems
):
    p = pl.program_id(0)
    me = here[0]
    buddy = swapped(me)[0]
    low = jnp.minimum(me, buddy)
    fetches = [
        pltpu.make_async_copy(from_sibling, halo.at[pl.ds(0, s.rows), :], sems.at[0]),
        pltpu.make_async_copy(blocks, near_blocks, sems.at[1]),
        pltpu.make_async_copy(dens_in, dens_own, sems.at[2]),
    ]

    @pl.when(p == 0)
    def _():
        for fetch in fetches:
            fetch.start()
        dens[...] = jnp.zeros_like(dens)
        for k in range(s.pairs):
            wide[(me - low) * s.pairs + k] = own[k]
            unpack(s, sibling, k, wide.at[(buddy - low) * s.pairs + k])

    right_col = column_of(pao_rows, partner[me * s.pairs + p])
    left_col = column_of(pao_rows, me * s.occ + lax.rem(p, s.occ))
    left_rows = []
    for c in range(ncpl):
        m = listed[c, p]
        spot = m - low * s.pairs
        inside = (spot >= 0) & (spot < 2 * s.pairs)
        weight = jnp.where(inside, coef[c, p], 0.0)
        left_rows.append(row_of(pao_rows, s.first_orbital(m)))
        right_row = row_of(pao_rows, partner[m]).astype(jnp.int16)
        moved = dot(wide[jnp.clip(spot, 0, 2 * s.pairs - 1)], same(right_col, right_row), NT)
        tall[c * s.pao : (c + 1) * s.pao] = (weight * moved).astype(jnp.bfloat16)
    left_row = jnp.concatenate(left_rows, axis=1).astype(jnp.int16)
    coupling[0] = dot(same(left_col, left_row), tall[...])

    for side in range(2):
        m = (low + side) * s.pairs + p
        near = partner[m] - me * s.occ

        @pl.when((near >= 0) & (near < s.occ))
        def _():
            masked = kept(wide[side * s.pairs + p], lens[s.first_orbital(m)], lens[partner[m]])
            dens[near] += dot(masked, masked, TN)

    @pl.when(p == 0)
    def _():
        for fetch in fetches:
            fetch.wait()

    right = partner[me * s.pairs + p]
    l, kind = s.where_partner(me, right)

    @pl.when(kind == 2)
    def _():
        exchange[0] = dot(aligned[0], near_blocks[lax.rem(right, s.occ)], NT)

    @pl.when(kind == 0)
    def _():
        usual = s.aux - 2 * LANES
        use = functools.partial(
            compacted, s, counts[l], offsets[l], rows_of(lens[right]), aligned.at[0], halo
        )
        exchange[0] = use(0, usual)

        @pl.when(counts[l] > usual)
        def _():
            exchange[0] += use(usual, s.aux)

    @pl.when(p == s.pairs - 1)
    def _():
        dens[...] = (dens[...] + dens_own[...]) * (1.0 / s.pao)


def far_kernel(
    s, ncpl, here, partner, listed, lens, coef, pao_rows, gaps, other, own, near_coupling, exchange, near_dens, coupling, halves, dens, new_amps, energy, wide, news, whose, which, sems
):
    me = here[0]
    device = swapped(me)[1]
    dens[...] = near_dens[...]
    coupling[...] = near_coupling[...]
    for k in range(s.pairs):
        unpack(s, other, k, wide.at[k])

    number = jnp.int32(0)
    for p in range(s.pairs):
        for c in range(ncpl):
            spot = listed[c, p] - device * s.pairs
            whose[number] = p
            which[number] = c
            number += ((spot >= 0) & (spot < s.pairs)).astype(jnp.int32)

    def term(n):
        weight = jnp.where(n < number, 1.0, 0.0)
        n = jnp.minimum(n, number - 1)
        p, c = whose[n], which[n]
        m = listed[c, p]
        right_col = column_of(pao_rows, partner[me * s.pairs + p])
        left_col = column_of(pao_rows, me * s.occ + lax.rem(p, s.occ))
        right_row = row_of(pao_rows, partner[m]).astype(jnp.int16)
        left_row = row_of(pao_rows, s.first_orbital(m)).astype(jnp.int16)
        moved = dot(wide[m - device * s.pairs], same(right_col, right_row), NT)
        return p, weight * coef[c, p] * dot(same(left_col, left_row), moved.astype(jnp.bfloat16))

    def some(n, _):
        terms = [term(2 * n), term(2 * n + 1)]
        for p, value in terms:
            coupling[p] += value
        return 0

    lax.fori_loop(0, (number + 1) // 2, some, 0)

    for k in range(s.pairs):
        m = device * s.pairs + k
        inside = (m >= 0) & (m < s.npair)
        m = jnp.clip(m, 0, s.npair - 1)
        near = partner[m] - me * s.occ

        @pl.when(inside & (near >= 0) & (near < s.occ))
        def _():
            masked = kept(wide[k], lens[s.first_orbital(m)], lens[partner[m]])
            dens[near] += dot(masked, masked, TN) * (1.0 / s.pao)

    def result(p):
        return pltpu.make_async_copy(news.at[p], new_amps.at[p], sems.at[p])

    def finish(p, _):
        left, right = me * s.occ + lax.rem(p, s.occ), partner[me * s.pairs + p]
        kind = s.where_partner(me, right)[1]
        energy[p] = 0.0

        @pl.when(kind != 1)
        def _():
            news[p], energy[p] = update(
                s, lens[left], lens[right], exchange[p], own[p], coupling[p], gaps[pl.ds(left, 1), :], gaps[pl.ds(right, 1), :]
            )
            result(p).start()

        @pl.when(kind == 1)
        def _():
            coupling[p], halves[p] = ready(
                s, lens[left], lens[right], own[p], coupling[p], gaps[pl.ds(left, 1), :], gaps[pl.ds(right, 1), :]
            )

        return 0

    def wait(p, _):
        kind = s.where_partner(me, partner[me * s.pairs + p])[1]
        pl.when(kind != 1)(result(p).wait)
        return 0

    lax.fori_loop(0, s.pairs, finish, 0)
    lax.fori_loop(0, s.pairs, wait, 0)


def update(s, lens_left, lens_right, exchange, amp, coupling, gap_left, gap_right):
    left = column(gap_left)
    parts = []
    energy = jnp.zeros((s.pao, LANES), jnp.float32)
    for at in range(0, s.pao, LANES):
        lanes = slice(at, min(at + LANES, s.pao))
        part = amp[:, lanes].astype(jnp.float32)
        shape = part.shape
        mask = live(lens_left, lens_right - at, shape)
        denom = left[:, : shape[1]] + gap_right[:, lanes]
        inverse = pl.reciprocal(denom, approx=True)
        inverse = inverse * (2.0 - denom * inverse)
        moved = (exchange[:, lanes] - coupling[:, lanes]) * inverse
        parts.append(jnp.where(mask, 0.5 * (part - moved), 0.0).astype(jnp.bfloat16))
        term = jnp.where(mask, exchange[:, lanes] * part, 0.0)
        if shape[1] < LANES:
            term = jnp.concatenate([term, jnp.zeros((s.pao, LANES - shape[1]), jnp.float32)], axis=1)
        energy += term
    return jnp.concatenate(parts, axis=1), jnp.sum(energy) / s.pao


def ready(s, lens_left, lens_right, amp, coupling, gap_left, gap_right):
    left = column(gap_left)
    bases, halves = [], []
    for at in range(0, s.pao, LANES):
        lanes = slice(at, min(at + LANES, s.pao))
        part = amp[:, lanes].astype(jnp.float32)
        mask = live(lens_left, lens_right - at, part.shape)
        denom = left[:, : part.shape[1]] + gap_right[:, lanes]
        inverse = pl.reciprocal(denom, approx=True)
        inverse = inverse * (2.0 - denom * inverse)
        halves.append(jnp.where(mask, 0.5 * inverse, 0.0))
        bases.append(jnp.where(mask, 0.5 * (part + coupling[:, lanes] * inverse), 0.0))
    return jnp.concatenate(bases, axis=1), jnp.concatenate(halves, axis=1)


def compacted(s, count, at, step, aligned, halo, low, high):
    parts = []
    for c in range(low // LANES, high // LANES):
        spot = pl.multiple_of(jnp.minimum(at + c * step, halo.shape[0] - s.pao), 16)
        part = halo[pl.ds(spot, s.pao), :]
        parts.append(jnp.where(c * LANES < count, part, jnp.zeros_like(part)))
    return dot(aligned[:, low:high], jnp.concatenate(parts, axis=1), NT)


def last_kernel(s, beyond, here, partner, lens, counts, offsets, energy_in, halves, aligned, bases, amps, other, *refs):
    if beyond:
        more, _, new_amps, energy, halo, news, sums, far, sems = refs
        halo[: s.first] = other[...]
        rest = pltpu.make_async_copy(
            more, halo.at[pl.ds(s.first, s.rows - s.first)], sems.at[s.pairs]
        )
        rest.start()
        rest.wait()
    else:
        _, new_amps, energy, news, sums, far, sems = refs
        halo = other
    me = here[0]

    def result(n):
        return pltpu.make_async_copy(news.at[n], new_amps.at[far[n]], sems.at[n])

    number = jnp.int32(0)
    for p in range(s.pairs):
        energy[p] = energy_in[p]
        far[number] = p
        kind = s.where_partner(me, partner[me * s.pairs + p])[1]
        number += (kind == 1).astype(jnp.int32)

    usual = s.aux - 2 * LANES

    def pair_of(n):
        p = far[jnp.minimum(n, number - 1)]
        right = partner[me * s.pairs + p]
        return p, right, s.occ + lax.rem(right, s.occ)

    def some(n, _):
        pairs = [pair_of(2 * n + t) for t in range(2)]
        for t, (p, right, l) in enumerate(pairs):
            sums[t] = compacted(s, counts[l], offsets[l], rows_of(lens[right]), aligned.at[p], halo, 0, usual)
        for t, (p, right, l) in enumerate(pairs):

            @pl.when(counts[l] > usual)
            def _():
                sums[t] += compacted(
                    s, counts[l], offsets[l], rows_of(lens[right]), aligned.at[p], halo, usual, s.aux
                )

        for t, (p, right, l) in enumerate(pairs):
            exchange, half = sums[t], halves[p]
            news[2 * n + t] = (bases[p] - exchange * half).astype(jnp.bfloat16)
            product = jnp.where(half > 0.0, exchange * amps[p].astype(jnp.float32), 0.0)
            energy[p] = jnp.sum(product) / s.pao
        for t in range(2):
            pl.when(2 * n + t < number)(result(2 * n + t).start)
        return 0

    def wait(n, _):
        result(n).wait()
        return 0

    lax.fori_loop(0, (number + 1) // 2, some, 0)
    lax.fori_loop(0, number, wait, 0)


def position():
    return lax.axis_index(AXES)


def swap(array, role):
    count = 1
    for axis in AXES:
        count *= lax.axis_size(axis)
    route = []
    for low in range(role, count - 1, 2):
        route += [(low, low + 1), (low + 1, low)]
    return lax.ppermute(array, AXES, route)


def run(
    beyond, blocks, aux_domain, pao_domain, pao_gap, amplitudes, pair_partner, coupling_list, coupling_coef
):
    s = Sizes(blocks, amplitudes, pair_partner)
    ncpl = coupling_list.shape[1]
    me = position()
    here = me.astype(jnp.int32).reshape(1)
    blocks_t = jnp.swapaxes(blocks, 1, 2)

    smem = pl.BlockSpec(memory_space=pltpu.SMEM)
    vmem = pl.BlockSpec(memory_space=pltpu.VMEM)
    pinned = pl.BlockSpec(memory_space=pltpu.HBM)
    anywhere = pl.BlockSpec(memory_space=pl.ANY)
    plain = pltpu.CompilerParams(vmem_limit_bytes=24 * MIB)
    stepped = pltpu.CompilerParams(
        dimension_semantics=("arbitrary",), vmem_limit_bytes=30 * MIB
    )
    alone = pltpu.CompilerParams(vmem_limit_bytes=34 * MIB)
    square = pl.BlockSpec((1, s.pao, s.pao), lambda p, *_: (p, 0, 0))
    all_dens = pl.BlockSpec((s.occ, s.pao, s.pao), lambda p, *_: (0, 0, 0))
    squares = jax.ShapeDtypeStruct((s.pairs, s.pao, s.pao), jnp.float32)
    dens_shape = jax.ShapeDtypeStruct((s.occ, s.pao, s.pao), jnp.float32)

    def cost(work, data):
        return pl.CostEstimate(flops=work, bytes_accessed=data, transcendentals=0)

    whole, tail, share = packing(s)
    slots = s.pairs + s.pairs // share
    slim = pl.pallas_call(
        functools.partial(slim_kernel, s),
        in_specs=[vmem],
        out_specs=vmem,
        out_shape=jax.ShapeDtypeStruct((slots, s.pao, whole), jnp.bfloat16),
        compiler_params=plain,
        cost_estimate=cost(10**6, 4 * 10**6),
        name="slim",
    )(amplitudes)
    amps_other = swap(slim, 1)
    amps_sibling = swap(slim, 0)

    lens = jnp.sum((pao_domain >= 0).astype(jnp.int32), axis=1)

    lists = 3 * s.occ
    to_sibling, to_other, to_other_more, tables, pao_rows, gap_rows, counts, offsets = pl.pallas_call(
        functools.partial(pack_kernel, s),
        in_specs=[smem] * 3 + [vmem] * 4 + [anywhere],
        out_specs=[pinned] * 3 + [vmem] * 3 + [smem] * 2,
        out_shape=[
            jax.ShapeDtypeStruct((s.rows, LANES), jnp.bfloat16),
            jax.ShapeDtypeStruct((s.first, LANES), jnp.bfloat16),
            jax.ShapeDtypeStruct((s.rows - s.first, LANES), jnp.bfloat16),
            jax.ShapeDtypeStruct((3, 2 * LOW, s.occ * HIGH), jnp.bfloat16),
            jax.ShapeDtypeStruct(pao_domain.shape, pao_domain.dtype),
            jax.ShapeDtypeStruct(pao_gap.shape, pao_gap.dtype),
            jax.ShapeDtypeStruct((lists,), jnp.int32),
            jax.ShapeDtypeStruct((lists,), jnp.int32),
        ],
        scratch_shapes=[
            pltpu.VMEM((3, 2 * LOW, s.occ * HIGH), jnp.float32),
            pltpu.VMEM((3 * s.occ, 2 * LOW, s.occ * HIGH), jnp.float32),
            pltpu.VMEM((2, 2 * LOW, s.occ * HIGH), jnp.bfloat16),
            pltpu.SMEM((s.occ,), jnp.int32),
            pltpu.VMEM((2, s.rows + s.pao, LANES), jnp.bfloat16),
            pltpu.SemaphoreType.DMA((3,)),
        ],
        compiler_params=plain,
        cost_estimate=cost(10**11, 10**5),
        name="pack",
    )(here, pair_partner, lens, aux_domain, blocks_t, pao_domain.T, pao_gap.T, slim)

    repeats = s.pairs // s.occ
    both = pl.BlockSpec((repeats, 1, s.pao, s.aux), lambda g: (0, g, 0, 0))
    aligned, dens, to_other, to_sibling = pl.pallas_call(
        functools.partial(own_kernel, s),
        grid=(s.occ,),
        in_specs=[smem] * 4
        + [
            vmem,
            vmem,
            pl.BlockSpec((1, s.pao, s.aux), lambda g: (g, 0, 0)),
            pl.BlockSpec((repeats, 1, s.pao, s.pao), lambda g: (0, g, 0, 0)),
            anywhere,
            anywhere,
        ],
        out_specs=[both, pl.BlockSpec((1, s.pao, s.pao), lambda g: (g, 0, 0)), anywhere, anywhere],
        out_shape=[
            jax.ShapeDtypeStruct((repeats, s.occ, s.pao, s.aux), jnp.bfloat16),
            dens_shape,
            jax.ShapeDtypeStruct(to_other.shape, to_other.dtype),
            jax.ShapeDtypeStruct(to_sibling.shape, to_sibling.dtype),
        ],
        input_output_aliases={8: 2, 9: 3},
        compiler_params=stepped,
        cost_estimate=cost(10**11, 10**5),
        name="own",
    )(
        here, pair_partner, lens, counts, tables, aux_domain, blocks_t,
        amplitudes.reshape(repeats, s.occ, s.pao, s.pao), to_other, to_sibling,
    )
    from_other = swap(to_other, 1)
    from_sibling = swap(to_sibling, 0)
    aligned = aligned.reshape(s.pairs, s.pao, s.aux)

    (over,) = pl.pallas_call(
        functools.partial(count_kernel, s),
        in_specs=[smem] * 2 + [vmem, anywhere],
        out_specs=[smem],
        out_shape=[jax.ShapeDtypeStruct((1,), jnp.int32)],
        compiler_params=plain,
        cost_estimate=cost(10**11, 10**5),
        name="count",
    )(pair_partner, lens, aux_domain, dens)

    coupling, exchange, dens = pl.pallas_call(
        functools.partial(near_kernel, s, ncpl),
        grid=(s.pairs,),
        in_specs=[smem] * 8
        + [vmem] * 3
        + [pl.BlockSpec((1, s.pao, s.aux), lambda p: (p, 0, 0))]
        + [anywhere, pinned, anywhere],
        out_specs=[square, square, all_dens],
        out_shape=[squares, squares, dens_shape],
        scratch_shapes=[
            pltpu.VMEM((2 * s.pairs, s.pao, s.pao), jnp.bfloat16),
            pltpu.VMEM((ncpl * s.pao, s.pao), jnp.bfloat16),
            pltpu.VMEM((s.occ, s.pao, s.pao), jnp.float32),
            pltpu.VMEM((s.occ, s.pao, s.aux), jnp.bfloat16),
            pltpu.VMEM((s.rows + s.pao, LANES), jnp.bfloat16),
            pltpu.SemaphoreType.DMA((3,)),
        ],
        compiler_params=stepped,
        cost_estimate=cost(10**11, 10**5),
        name="near",
    )(
        here, pair_partner, coupling_list.T, lens, coupling_coef.T, counts, offsets, over,
        pao_rows, amps_sibling, amplitudes, aligned, dens, blocks_t, from_sibling,
    )

    bases, halves, densities, some_amps, some_energies = pl.pallas_call(
        functools.partial(far_kernel, s, ncpl),
        in_specs=[smem] * 5 + [vmem] * 7,
        out_specs=[vmem, vmem, vmem, pinned, smem],
        out_shape=[
            squares,
            squares,
            dens_shape,
            jax.ShapeDtypeStruct(amplitudes.shape, amplitudes.dtype),
            jax.ShapeDtypeStruct((s.pairs,), jnp.float32),
        ],
        scratch_shapes=[
            pltpu.VMEM((s.pairs, s.pao, s.pao), jnp.bfloat16),
            pltpu.VMEM((s.pairs, s.pao, s.pao), jnp.bfloat16),
            pltpu.SMEM((s.pairs * ncpl,), jnp.int32),
            pltpu.SMEM((s.pairs * ncpl,), jnp.int32),
            pltpu.SemaphoreType.DMA((s.pairs,)),
        ],
        compiler_params=alone,
        cost_estimate=cost(10**10, 10**5),
        name="far",
    )(
        here, pair_partner, coupling_list.T, lens, coupling_coef.T,
        pao_rows, gap_rows, amps_other, amplitudes, coupling, exchange, dens,
    )

    more = (swap(to_other_more, 1),) if beyond else ()
    scratch = [
        pltpu.VMEM((s.pairs, s.pao, s.pao), jnp.bfloat16),
        pltpu.VMEM((2, s.pao, s.pao), jnp.float32),
        pltpu.SMEM((s.pairs,), jnp.int32),
        pltpu.SemaphoreType.DMA((s.pairs + 1,)),
    ]
    if beyond:
        scratch = [pltpu.VMEM((s.rows + s.pao, LANES), jnp.bfloat16)] + scratch
    new_amps, energies = pl.pallas_call(
        functools.partial(last_kernel, s, beyond),
        in_specs=[smem] * 6 + [vmem] * 5 + [pinned] * (len(more) + 1),
        out_specs=[pinned, smem],
        out_shape=[
            jax.ShapeDtypeStruct(amplitudes.shape, amplitudes.dtype),
            jax.ShapeDtypeStruct((s.pairs,), jnp.float32),
        ],
        scratch_shapes=scratch,
        input_output_aliases={11 + len(more): 0},
        compiler_params=alone,
        cost_estimate=cost(2 * s.pairs * s.pao * s.pao * s.aux, 2 * 10**7),
        name="last",
    )(
        here, pair_partner, lens, counts, offsets, some_energies,
        halves, aligned, bases, amplitudes, from_other, *more, some_amps,
    )
    return new_amps, energies, densities, over


def local(*arrays):
    new_amps, energies, densities, over = run(False, *arrays)
    new_amps, energies = lax.cond(
        over[0] > 0, lambda ops: run(True, *ops[2:])[:2], lambda ops: ops[:2], (new_amps, energies) + arrays
    )
    return (new_amps, energies, densities)


def solution(mesh):
    return jax.shard_map(
        local,
        mesh=mesh,
        in_specs=(
            P(AXES, None, None),
            P(),
            P(),
            P(),
            P(AXES, None, None),
            P(),
            P(AXES, None),
            P(AXES, None),
        ),
        out_specs=(P(AXES, None, None), P(AXES), P(AXES, None, None)),
        check_vma=False,
    )
```

profile of v0, /device:TPU:9, one launch (start us, length us, event | category | flops | bytes accessed | tf_op | source)
XLA Modules:
  0.0 92.4 jit_solution(13894834588906350198)
XLA Ops:
  0.6 0.0 copy-start.8
  0.6 0.0 copy-start.10
  0.7 0.0 copy-start.13
  0.7 0.0 copy-start.14
  0.7 3.0 %slim.3._ = bf16[10,320,256]{2,1,0:T(8,128)(2,1)} custom-call(bf16[8,320,320]{2,1,0:T(8,128)(2,1)} %amps.3), custom_call_target="tpu_custom_call" | custom-call | flops 1000000 | bytes 4000000 | tf_op jit(solution)/shard_map/slim/pallas_call | solution.py:646
  3.6 0.7 collective-permute-start.6
  4.3 3.0 %collective-permute-start.5 = (bf16[10,320,256]{2,1,0:T(8,128)(2,1)}, bf16[10,320,256]{2,1,0:T(8,128)(2,1)}, u32[]{:S(2)}, u32[]{:S(2)}) collective-permute-start(bf16[10,320,256]{2,1,0:T(8,128)(2,1)} %slim.3._), channel_id=1, source_target_pairs={{1,2},{2,1},{3,4},{4,3},{5,6},{6,5},{7,8},{8,7},{9,10},{10,9},{11,... | collective-permute-start | bytes 4915208 | tf_op jit(solution)/shard_map/ppermute | solution.py:615
  7.3 0.0 copy-done.8
  7.3 0.1 convert_reduce_fusion.1.lens
  7.4 0.0 copy-done.10
  7.4 0.0 copy-done.13
  7.4 0.0 copy-done.14
  7.4 0.0 copy-start.7
  7.4 0.0 copy-start.11
  7.4 12.1 %pack.3 = (bf16[10240,128]{1,0:T(8,128)(2,1)S(1)}, bf16[6400,128]{1,0:T(8,128)(2,1)}, bf16[3840,128]{1,0:T(8,128)(2,1)}, bf16[3,128,128]{2,1,0:T(8,128)(2,1)S(1)...) custom-call(s32[1]{0:T(128)} %bitcast.8.here, s32[256]{0:T(256)S(1)} %copy-done.10, ...), custom_call_target="tpu_custom_call" | custom-call | flops 99999997952 | bytes 100000 | tf_op jit(solution)/shard_map/pack/pallas_call | solution.py:661
  19.5 0.0 copy-done.7
  19.5 0.0 copy-done.11
  19.5 9.1 %own.5 = (bf16[2,4,320,1024]{3,2,1,0:T(8,128)(2,1)S(1)}, f32[4,320,320]{2,1,0:T(8,128)S(1)}, bf16[6400,128]{1,0:T(8,128)(2,1)}, bf16[10240,128]{1,0:T(8,128)(2,1)S(1)}) custom-call(s32[1]{0:T(128)} %bitcast.8.here, s32[256]{0:T(256)S(1)} %copy-done.10, s32[128]{0:T(128)S(1)} %convert_reduce_fusion.1.lens, ...), custom_call_target="tpu_custom_call", output_to_operand_aliasing={{2}: (8, {}), {3}: (9, {})} | custom-call | flops 99999997952 | bytes 100000 | tf_op jit(solution)/shard_map/own/pallas_call | solution.py:690
  28.6 1.9 %collective-permute-start.8 = (bf16[6400,128]{1,0:T(8,128)(2,1)}, bf16[6400,128]{1,0:T(8,128)(2,1)}, u32[]{:S(2)}, u32[]{:S(2)}) collective-permute-start(bf16[6400,128]{1,0:T(8,128)(2,1)} %get-tuple-element.87), channel_id=1, source_target_pairs={{1,2},{2,1},{3,4},{4,3},{5,6},{6,5},{7,8},{8,7},{9,10},{10,9},{11,... | collective-permute-start | bytes 4915208 | tf_op jit(solution)/shard_map/ppermute | solution.py:615
  30.5 4.7 %collective-permute-start.7 = (bf16[10240,128]{1,0:T(8,128)(2,1)S(1)}, bf16[10240,128]{1,0:T(8,128)(2,1)S(1)}, u32[]{:S(2)}, u32[]{:S(2)}) collective-permute-start(bf16[10240,128]{1,0:T(8,128)(2,1)S(1)} %get-tuple-element.80), channel_id=1, source_target_pairs={{0,1},{1,0},{2,3},{3,2},{4,5},{5,4},{6,7},{7,6},{8,9},{9,8},{10,11... | collective-permute-start | bytes 7864328 | tf_op jit(solution)/shard_map/ppermute | solution.py:615
  35.3 0.0 copy-start.16
  35.3 0.0 copy-start.18
  35.3 7.3 %count.3._ = s32[1]{0:T(128)} custom-call(s32[256]{0:T(256)S(1)} %copy-done.10, s32[128]{0:T(128)S(1)} %convert_reduce_fusion.1.lens, s32[128,1024]{1,0:T(8,128)S(1)} %copy-done.13, f32[4,320,320]{2,1,0:T(8,128)S(1)} %get-tuple-element.75._.dens_in), custom_call_target="tpu_custom_call" | custom-call | flops 99999997952 | bytes 100000 | tf_op jit(solution)/shard_map/count/pallas_call | solution.py:721
  43.2 0.0 collective-permute-done.6.sibling
  43.2 0.0 collective-permute-done.7.from_sibling
  43.2 0.0 copy-done.16
  43.3 0.0 copy-done.18
  43.3 18.0 %near.3 = (f32[8,320,320]{2,1,0:T(8,128)S(1)}, f32[8,320,320]{2,1,0:T(8,128)S(1)}, f32[4,320,320]{2,1,0:T(8,128)S(1)}) custom-call(s32[1]{0:T(128)} %bitcast.8.here, s32[256]{0:T(256)S(1)} %copy-done.10, s32[4,8]{1,0:T(4,128)S(1)} %bitcast.33, s32[128]{0:T(128)S(1)} %convert_reduce_fusion.1.lens, f32[4,8]{1,0:T(4,128)S(1)} %bitcast.37, ...), custom_call_target="tpu_custom_call" | custom-call | flops 99999997952 | bytes 100000 | tf_op jit(solution)/shard_map/near/pallas_call | solution.py:731
  61.3 0.0 copy-start.3
  61.3 1.9 %copy-done.3 = f32[8,320,320]{2,1,0:T(8,128)} copy-done((f32[8,320,320]{2,1,0:T(8,128)}, f32[8,320,320]{2,1,0:T(8,128)S(1)}, u32[]{:S(2)}) %copy-start.3) | copy-done | bytes 3276824
  63.2 0.0 copy-start.5
  63.2 1.9 %copy-done.5 = f32[8,320,320]{2,1,0:T(8,128)} copy-done((f32[8,320,320]{2,1,0:T(8,128)}, f32[8,320,320]{2,1,0:T(8,128)S(1)}, u32[]{:S(2)}) %copy-start.5) | copy-done | bytes 3276824
  65.0 0.0 collective-permute-done.5.other
  65.0 0.0 copy-start.4
  65.1 2.1 %copy-done.4 = f32[8,320,320]{2,1,0:T(8,128)S(1)} copy-done((f32[8,320,320]{2,1,0:T(8,128)S(1)}, f32[8,320,320]{2,1,0:T(8,128)}, u32[]{:S(2)}) %copy-start.4) | copy-done | bytes 3276824
  67.2 0.0 copy-start.6
  67.2 2.1 %copy-done.6 = f32[8,320,320]{2,1,0:T(8,128)S(1)} copy-done((f32[8,320,320]{2,1,0:T(8,128)S(1)}, f32[8,320,320]{2,1,0:T(8,128)}, u32[]{:S(2)}) %copy-start.6) | copy-done | bytes 3276824
  69.3 17.5 %far.3 = (f32[8,320,320]{2,1,0:T(8,128)S(1)}, f32[8,320,320]{2,1,0:T(8,128)S(1)}, f32[4,320,320]{2,1,0:T(8,128)}, bf16[8,320,320]{2,1,0:T(8,128)(2,1)}, f32[8]{0:T(128)S(1)}) custom-call(s32[1]{0:T(128)} %bitcast.8.here, s32[256]{0:T(256)S(1)} %copy-done.10, s32[4,8]{1,0:T(4,128)S(1)} %bitcast.34, s32[128]{0:T(128)S(1)} %convert_reduce_fusion.1.lens, ...), custom_call_target="tpu_custom_call" | custom-call | flops 10000000000 | bytes 100000 | tf_op jit(solution)/shard_map/far/pallas_call | solution.py:756
  86.8 0.0 collective-permute-done.8.other
  86.8 0.0 copy-start.9
  86.8 0.0 copy-start.15
  86.8 5.4 %last.3 = (bf16[8,320,320]{2,1,0:T(8,128)(2,1)}, f32[8]{0:T(128)}) custom-call(s32[1]{0:T(128)} %bitcast.8.here, s32[256]{0:T(256)S(1)} %copy-done.10, s32[128]{0:T(128)S(1)} %convert_reduce_fusion.1.lens, s32[12]{0:T(128)S(1)} %get-tuple-element.71.counts, s32[12]{0:T(128)S(1)} %get-tuple-element.76.offsets, ...), custom_call_target="tpu_custom_call", output_to_operand_aliasing={{0}: (11, {})} | custom-call | flops 1677721600 | bytes 20000000 | tf_op jit(solution)/shard_map/last/pallas_call | solution.py:791
  92.2 0.0 copy-done.9
  92.2 0.0 copy-done.15
  (1 shorter events, 0.0 us)
Async XLA Ops:
  0.6 6.7 %copy-start.8 = (s32[128,320]{0,1:T(8,128)S(1)}, s32[128,320]{0,1:T(8,128)}, u32[]{:S(2)}) copy-start(s32[128,320]{0,1:T(8,128)} %param.12) | copy-start | bytes 491524
  0.6 6.8 %copy-start.10 = (s32[256]{0:T(256)S(1)}, s32[256]{0:T(256)}, u32[]{:S(2)}) copy-start(s32[256]{0:T(256)} %partner.11) | copy-start | bytes 3076
  0.7 6.8 %copy-start.13 = (s32[128,1024]{1,0:T(8,128)S(1)}, s32[128,1024]{1,0:T(8,128)}, u32[]{:S(2)}) copy-start(s32[128,1024]{1,0:T(8,128)} %aux_rows.5) | copy-start | bytes 1572868
  0.7 6.8 %copy-start.14 = (f32[128,320]{0,1:T(8,128)S(1)}, f32[128,320]{0,1:T(8,128)}, u32[]{:S(2)}) copy-start(f32[128,320]{0,1:T(8,128)} %param.13) | copy-start | bytes 491524
  3.6 39.6 %collective-permute-start.6 = (bf16[10,320,256]{2,1,0:T(8,128)(2,1)}, bf16[10,320,256]{2,1,0:T(8,128)(2,1)}, u32[]{:S(2)}, u32[]{:S(2)}) collective-permute-start(bf16[10,320,256]{2,1,0:T(8,128)(2,1)} %slim.3._), channel_id=1, source_target_pairs={{0,1},{1,0},{2,3},{3,2},{4,5},{5,4},{6,7},{7,6},{8,9},{9,8},{10,11... | collective-permute-start | bytes 4915208 | tf_op jit(solution)/shard_map/ppermute | solution.py:615
  4.3 60.7 %collective-permute-start.5 = (bf16[10,320,256]{2,1,0:T(8,128)(2,1)}, bf16[10,320,256]{2,1,0:T(8,128)(2,1)}, u32[]{:S(2)}, u32[]{:S(2)}) collective-permute-start(bf16[10,320,256]{2,1,0:T(8,128)(2,1)} %slim.3._), channel_id=1, source_target_pairs={{1,2},{2,1},{3,4},{4,3},{5,6},{6,5},{7,8},{8,7},{9,10},{10,9},{11,... | collective-permute-start | bytes 4915208 | tf_op jit(solution)/shard_map/ppermute | solution.py:615
  7.4 12.1 %copy-start.7 = (bf16[8,320,320]{2,1,0:T(8,128)(2,1)S(1)}, bf16[8,320,320]{2,1,0:T(8,128)(2,1)}, u32[]{:S(2)}) copy-start(bf16[8,320,320]{2,1,0:T(8,128)(2,1)} %amps.3) | copy-start | bytes 4915204
  7.4 12.1 %copy-start.11 = (bf16[4,1024,320]{1,2,0:T(8,128)(2,1)S(1)}, bf16[4,1024,320]{1,2,0:T(8,128)(2,1)}, u32[]{:S(2)}) copy-start(bf16[4,1024,320]{1,2,0:T(8,128)(2,1)} %param.10) | copy-start | bytes 7864324
  28.6 58.1 %collective-permute-start.8 = (bf16[6400,128]{1,0:T(8,128)(2,1)}, bf16[6400,128]{1,0:T(8,128)(2,1)}, u32[]{:S(2)}, u32[]{:S(2)}) collective-permute-start(bf16[6400,128]{1,0:T(8,128)(2,1)} %get-tuple-element.87), channel_id=1, source_target_pairs={{1,2},{2,1},{3,4},{4,3},{5,6},{6,5},{7,8},{8,7},{9,10},{10,9},{11,... | collective-permute-start | bytes 4915208 | tf_op jit(solution)/shard_map/ppermute | solution.py:615
  30.5 12.7 %collective-permute-start.7 = (bf16[10240,128]{1,0:T(8,128)(2,1)S(1)}, bf16[10240,128]{1,0:T(8,128)(2,1)S(1)}, u32[]{:S(2)}, u32[]{:S(2)}) collective-permute-start(bf16[10240,128]{1,0:T(8,128)(2,1)S(1)} %get-tuple-element.80), channel_id=1, source_target_pairs={{0,1},{1,0},{2,3},{3,2},{4,5},{5,4},{6,7},{7,6},{8,9},{9,8},{10,11... | collective-permute-start | bytes 7864328 | tf_op jit(solution)/shard_map/ppermute | solution.py:615
  35.3 8.0 %copy-start.16 = (s32[8,4]{0,1:T(4,128)S(1)}, s32[8,4]{0,1:T(4,128)}, u32[]{:S(2)}) copy-start(s32[8,4]{0,1:T(4,128)} %param.16) | copy-start | bytes 388
  35.3 8.0 %copy-start.18 = (f32[8,4]{0,1:T(4,128)S(1)}, f32[8,4]{0,1:T(4,128)}, u32[]{:S(2)}) copy-start(f32[8,4]{0,1:T(4,128)} %param.17) | copy-start | bytes 388
  61.3 1.9 %copy-start.3 = (f32[8,320,320]{2,1,0:T(8,128)}, f32[8,320,320]{2,1,0:T(8,128)S(1)}, u32[]{:S(2)}) copy-start(f32[8,320,320]{2,1,0:T(8,128)S(1)} %get-tuple-element.81.near_coupling) | copy-start | bytes 9830404
  63.2 1.9 %copy-start.5 = (f32[8,320,320]{2,1,0:T(8,128)}, f32[8,320,320]{2,1,0:T(8,128)S(1)}, u32[]{:S(2)}) copy-start(f32[8,320,320]{2,1,0:T(8,128)S(1)} %get-tuple-element.82.exchange) | copy-start | bytes 9830404
  65.0 2.1 %copy-start.4 = (f32[8,320,320]{2,1,0:T(8,128)S(1)}, f32[8,320,320]{2,1,0:T(8,128)}, u32[]{:S(2)}) copy-start(f32[8,320,320]{2,1,0:T(8,128)} %copy-done.3) | copy-start | bytes 9830404
  67.2 2.1 %copy-start.6 = (f32[8,320,320]{2,1,0:T(8,128)S(1)}, f32[8,320,320]{2,1,0:T(8,128)}, u32[]{:S(2)}) copy-start(f32[8,320,320]{2,1,0:T(8,128)} %copy-done.5) | copy-start | bytes 9830404
  86.8 5.4 %copy-start.9 = (s32[128,320]{0,1:T(8,128)S(1)}, s32[128,320]{0,1:T(8,128)}, u32[]{:S(2)}) copy-start(s32[128,320]{0,1:T(8,128)} %param.12) | copy-start | bytes 491524
  86.8 5.4 %copy-start.15 = (f32[128,320]{0,1:T(8,128)S(1)}, f32[128,320]{0,1:T(8,128)}, u32[]{:S(2)}) copy-start(f32[128,320]{0,1:T(8,128)} %param.13) | copy-start | bytes 491524
where the time goes:
time: 91.2 us; the launch traced here: 92.4 us
  Pallas kernels  72.3 us (79%)
  starting transfers between devices  10.3 us (11%)
  local copies, waits for them, and re-layouts  8.05 us (9%)
  between operations  1.69 us (2%)
    pallas_call x1, Pallas kernels, run(): pl.pallas_call(functools.partial(near_kernel, s, ncpl), grid=(s.pairs,),...  18 us
    pallas_call x1, Pallas kernels, run(): pl.pallas_call(functools.partial(far_kernel, s, ncpl), in_specs=[smem] *...  17.5 us
    pallas_call x1, Pallas kernels, run(): pl.pallas_call(functools.partial(pack_kernel, s), in_specs=[smem] * 3 + [...  12.1 us
    ppermute x4, starting transfers between devices, swap(): return lax.ppermute(array, AXES, route)  10.3 us
    pallas_call x1, Pallas kernels, run(): pl.pallas_call(functools.partial(own_kernel, s), grid=(s.occ,), in_specs=...  9.06 us
    unnamed x28, local copies, waits for them, and re-layouts  8.05 us
    pallas_call x1, Pallas kernels, run(): pl.pallas_call(functools.partial(count_kernel, s), in_specs=[smem] * 2 +...  7.29 us
    pallas_call x1, Pallas kernels, run(): pl.pallas_call(functools.partial(last_kernel, s, beyond), in_specs=[smem]...  5.39 us
  transfers between devices with their start and end apart: 4, of which 0 were waited for; matrix products, arithmetic and copies ran while one was open for 0% of the time, Pallas kernels for 69%

commit v1 on v0

--- a/solution.py
+++ b/solution.py
@@ -632,7 +632,7 @@
     stepped = pltpu.CompilerParams(
         dimension_semantics=("arbitrary",), vmem_limit_bytes=30 * MIB
     )
-    alone = pltpu.CompilerParams(vmem_limit_bytes=34 * MIB)
+    alone = pltpu.CompilerParams(vmem_limit_bytes=28 * MIB)
     square = pl.BlockSpec((1, s.pao, s.pao), lambda p, *_: (p, 0, 0))
     all_dens = pl.BlockSpec((s.occ, s.pao, s.pao), lambda p, *_: (0, 0, 0))
     squares = jax.ShapeDtypeStruct((s.pairs, s.pao, s.pao), jnp.float32)
@@ -771,6 +771,7 @@
             pltpu.SMEM((s.pairs * ncpl,), jnp.int32),
             pltpu.SemaphoreType.DMA((s.pairs,)),
         ],
+        input_output_aliases={9: 0},
         compiler_params=alone,
         cost_estimate=cost(10**10, 10**5),
         name="far",

time: 91.2 us -> 87.5 us (0.959)
  the two profiles are of different devices: /device:TPU:9 before, /device:TPU:27 now
where the time goes in v1:
time: 87.5 us; the launch traced here: 87.9 us
  Pallas kernels  68.5 us (78%)
  waiting for transfers between devices  9.05 us (10%)
  starting transfers between devices  8.57 us (10%)
  between operations  1.67 us (2%)
    pallas_call x1, Pallas kernels, run(): pl.pallas_call(functools.partial(near_kernel, s, ncpl), grid=(s.pairs,),...  17.8 us
    pallas_call x1, Pallas kernels, run(): pl.pallas_call(functools.partial(far_kernel, s, ncpl), in_specs=[smem] *...  13.9 us
    pallas_call x1, Pallas kernels, run(): pl.pallas_call(functools.partial(own_kernel, s), grid=(s.occ,), in_specs=...  10.6 us
    pallas_call x1, Pallas kernels, run(): pl.pallas_call(functools.partial(pack_kernel, s), in_specs=[smem] * 3 + [...  10.4 us
    ppermute x4, waiting for transfers between devices, swap(): return lax.ppermute(array, AXES, route)  9.05 us
    ppermute x4, starting transfers between devices, swap(): return lax.ppermute(array, AXES, route)  8.57 us
    pallas_call x1, Pallas kernels, run(): pl.pallas_call(functools.partial(last_kernel, s, beyond), in_specs=[smem]...  7.66 us
    pallas_call x1, Pallas kernels, run(): pl.pallas_call(functools.partial(count_kernel, s), in_specs=[smem] * 2 +...  5.09 us
  transfers between devices with their start and end apart: 4, of which 1 were waited for; matrix products, arithmetic and copies ran while one was open for 0% of the time, Pallas kernels for 66%

profile of v1, /device:TPU:27, one launch (start us, length us, event | category | flops | bytes accessed | tf_op | source)
XLA Modules:
  0.0 87.9 jit_solution(18209196474429350892)
XLA Ops:
  0.6 0.0 copy-start.3
  0.6 0.0 copy-start.5
  0.7 0.0 copy-start.6
  0.7 0.0 copy-start.7
  0.7 3.0 %slim.3._ = bf16[10,320,256]{2,1,0:T(8,128)(2,1)} custom-call(bf16[8,320,320]{2,1,0:T(8,128)(2,1)} %amps.3), custom_call_target="tpu_custom_call" | custom-call | flops 1000000 | bytes 4000000 | tf_op jit(solution)/shard_map/slim/pallas_call | solution.py:646
  3.6 0.7 collective-permute-start.6
  4.3 3.0 %collective-permute-start.5 = (bf16[10,320,256]{2,1,0:T(8,128)(2,1)}, bf16[10,320,256]{2,1,0:T(8,128)(2,1)}, u32[]{:S(2)}, u32[]{:S(2)}) collective-permute-start(bf16[10,320,256]{2,1,0:T(8,128)(2,1)} %slim.3._), channel_id=1, source_target_pairs={{1,2},{2,1},{3,4},{4,3},{5,6},{6,5},{7,8},{8,7},{9,10},{10,9},{11,... | collective-permute-start | bytes 4915208 | tf_op jit(solution)/shard_map/ppermute | solution.py:615
  7.3 0.0 copy-done.3
  7.3 0.1 convert_reduce_fusion.1.lens
  7.4 0.0 copy-done.5
  7.4 0.0 copy-done.6
  7.4 0.0 copy-done.7
  7.4 0.0 copy-start.2
  7.4 10.4 %pack.3 = (bf16[10240,128]{1,0:T(8,128)(2,1)S(1)}, bf16[6400,128]{1,0:T(8,128)(2,1)}, bf16[3840,128]{1,0:T(8,128)(2,1)}, bf16[3,128,128]{2,1,0:T(8,128)(2,1)S(1)...) custom-call(s32[1]{0:T(128)} %bitcast.8.here, s32[256]{0:T(256)S(1)} %copy-done.5, ...), custom_call_target="tpu_custom_call" | custom-call | flops 99999997952 | bytes 100000 | tf_op jit(solution)/shard_map/pack/pallas_call | solution.py:661
  17.9 0.0 copy-done.2
  17.9 10.6 %own.5 = (bf16[2,4,320,1024]{3,2,1,0:T(8,128)(2,1)S(1)}, f32[4,320,320]{2,1,0:T(8,128)S(1)}, bf16[6400,128]{1,0:T(8,128)(2,1)}, bf16[10240,128]{1,0:T(8,128)(2,1)S(1)}) custom-call(s32[1]{0:T(128)} %bitcast.8.here, s32[256]{0:T(256)S(1)} %copy-done.5, s32[128]{0:T(128)S(1)} %convert_reduce_fusion.1.lens, ...), custom_call_target="tpu_custom_call", output_to_operand_aliasing={{2}: (8, {}), {3}: (9, {})} | custom-call | flops 99999997952 | bytes 100000 | tf_op jit(solution)/shard_map/own/pallas_call | solution.py:690
  28.5 4.8 %collective-permute-start.8 = (bf16[6400,128]{1,0:T(8,128)(2,1)}, bf16[6400,128]{1,0:T(8,128)(2,1)}, u32[]{:S(2)}, u32[]{:S(2)}) collective-permute-start(bf16[6400,128]{1,0:T(8,128)(2,1)} %get-tuple-element.87), channel_id=1, source_target_pairs={{1,2},{2,1},{3,4},{4,3},{5,6},{6,5},{7,8},{8,7},{9,10},{10,9},{11,... | collective-permute-start | bytes 4915208 | tf_op jit(solution)/shard_map/ppermute | solution.py:615
  33.4 0.1 collective-permute-start.7
  33.5 0.0 copy-start.9
  33.5 0.0 copy-start.11
  33.5 5.1 %count.3._ = s32[1]{0:T(128)} custom-call(s32[256]{0:T(256)S(1)} %copy-done.5, s32[128]{0:T(128)S(1)} %convert_reduce_fusion.1.lens, s32[128,1024]{1,0:T(8,128)S(1)} %copy-done.6, f32[4,320,320]{2,1,0:T(8,128)S(1)} %get-tuple-element.75._.dens_in), custom_call_target="tpu_custom_call" | custom-call | flops 99999997952 | bytes 100000 | tf_op jit(solution)/shard_map/count/pallas_call | solution.py:721
  39.2 0.0 collective-permute-done.6.sibling
  39.2 0.0 collective-permute-done.7.from_sibling
  39.2 0.0 copy-done.9
  39.3 0.0 copy-done.11
  39.3 17.8 %near.3 = (f32[8,320,320]{2,1,0:T(8,128)S(1)}, f32[8,320,320]{2,1,0:T(8,128)S(1)}, f32[4,320,320]{2,1,0:T(8,128)S(1)}) custom-call(s32[1]{0:T(128)} %bitcast.8.here, s32[256]{0:T(256)S(1)} %copy-done.5, s32[4,8]{1,0:T(4,128)S(1)} %bitcast.27, s32[128]{0:T(128)S(1)} %convert_reduce_fusion.1.lens, f32[4,8]{1,0:T(4,128)S(1)} %bitcast.31, ...), custom_call_target="tpu_custom_call" | custom-call | flops 99999997952 | bytes 100000 | tf_op jit(solution)/shard_map/near/pallas_call | solution.py:731
  57.0 0.0 collective-permute-done.5.other
  57.1 13.9 %far.3 = (f32[8,320,320]{2,1,0:T(8,128)S(1)}, f32[8,320,320]{2,1,0:T(8,128)S(1)}, f32[4,320,320]{2,1,0:T(8,128)}, bf16[8,320,320]{2,1,0:T(8,128)(2,1)}, f32[8]{0:T(128)S(1)}) custom-call(s32[1]{0:T(128)} %bitcast.8.here, s32[256]{0:T(256)S(1)} %copy-done.5, s32[4,8]{1,0:T(4,128)S(1)} %bitcast.28, ...), custom_call_target="tpu_custom_call", output_to_operand_aliasing={{0}: (9, {})} | custom-call | flops 10000000000 | bytes 100000 | tf_op jit(solution)/shard_map/far/pallas_call | solution.py:756
  71.0 9.0 %collective-permute-done.8.other = bf16[6400,128]{1,0:T(8,128)(2,1)} collective-permute-done((bf16[6400,128]{1,0:T(8,128)(2,1)}, bf16[6400,128]{1,0:T(8,128)(2,1)}, u32[]{:S(2)}, u32[]{:S(2)}) %collective-permute-start.8) | collective-permute-done | bytes 1638432 | tf_op jit(solution)/shard_map/ppermute | solution.py:615
  80.0 0.0 copy-start.4
  80.0 0.0 copy-start.8
  80.0 7.7 %last.3 = (bf16[8,320,320]{2,1,0:T(8,128)(2,1)}, f32[8]{0:T(128)}) custom-call(s32[1]{0:T(128)} %bitcast.8.here, s32[256]{0:T(256)S(1)} %copy-done.5, s32[128]{0:T(128)S(1)} %convert_reduce_fusion.1.lens, s32[12]{0:T(128)S(1)} %get-tuple-element.71.counts, s32[12]{0:T(128)S(1)} %get-tuple-element.76.offsets, ...), custom_call_target="tpu_custom_call", output_to_operand_aliasing={{0}: (11, {})} | custom-call | flops 1677721600 | bytes 20000000 | tf_op jit(solution)/shard_map/last/pallas_call | solution.py:792
  87.7 0.0 copy-done.4
  87.7 0.0 copy-done.8
  (1 shorter events, 0.0 us)
Async XLA Ops:
  0.6 6.7 %copy-start.3 = (s32[128,320]{0,1:T(8,128)S(1)}, s32[128,320]{0,1:T(8,128)}, u32[]{:S(2)}) copy-start(s32[128,320]{0,1:T(8,128)} %param.12) | copy-start | bytes 491524
  0.6 6.8 %copy-start.5 = (s32[256]{0:T(256)S(1)}, s32[256]{0:T(256)}, u32[]{:S(2)}) copy-start(s32[256]{0:T(256)} %partner.11) | copy-start | bytes 3076
  0.7 6.8 %copy-start.6 = (s32[128,1024]{1,0:T(8,128)S(1)}, s32[128,1024]{1,0:T(8,128)}, u32[]{:S(2)}) copy-start(s32[128,1024]{1,0:T(8,128)} %aux_rows.5) | copy-start | bytes 1572868
  0.7 6.8 %copy-start.7 = (f32[128,320]{0,1:T(8,128)S(1)}, f32[128,320]{0,1:T(8,128)}, u32[]{:S(2)}) copy-start(f32[128,320]{0,1:T(8,128)} %param.13) | copy-start | bytes 491524
  3.6 35.6 %collective-permute-start.6 = (bf16[10,320,256]{2,1,0:T(8,128)(2,1)}, bf16[10,320,256]{2,1,0:T(8,128)(2,1)}, u32[]{:S(2)}, u32[]{:S(2)}) collective-permute-start(bf16[10,320,256]{2,1,0:T(8,128)(2,1)} %slim.3._), channel_id=1, source_target_pairs={{0,1},{1,0},{2,3},{3,2},{4,5},{5,4},{6,7},{7,6},{8,9},{9,8},{10,11... | collective-permute-start | bytes 4915208 | tf_op jit(solution)/shard_map/ppermute | solution.py:615
  4.3 52.7 %collective-permute-start.5 = (bf16[10,320,256]{2,1,0:T(8,128)(2,1)}, bf16[10,320,256]{2,1,0:T(8,128)(2,1)}, u32[]{:S(2)}, u32[]{:S(2)}) collective-permute-start(bf16[10,320,256]{2,1,0:T(8,128)(2,1)} %slim.3._), channel_id=1, source_target_pairs={{1,2},{2,1},{3,4},{4,3},{5,6},{6,5},{7,8},{8,7},{9,10},{10,9},{11,... | collective-permute-start | bytes 4915208 | tf_op jit(solution)/shard_map/ppermute | solution.py:615
  7.4 10.5 %copy-start.2 = (bf16[8,320,320]{2,1,0:T(8,128)(2,1)S(1)}, bf16[8,320,320]{2,1,0:T(8,128)(2,1)}, u32[]{:S(2)}) copy-start(bf16[8,320,320]{2,1,0:T(8,128)(2,1)} %amps.3) | copy-start | bytes 4915204
  28.5 51.4 %collective-permute-start.8 = (bf16[6400,128]{1,0:T(8,128)(2,1)}, bf16[6400,128]{1,0:T(8,128)(2,1)}, u32[]{:S(2)}, u32[]{:S(2)}) collective-permute-start(bf16[6400,128]{1,0:T(8,128)(2,1)} %get-tuple-element.87), channel_id=1, source_target_pairs={{1,2},{2,1},{3,4},{4,3},{5,6},{6,5},{7,8},{8,7},{9,10},{10,9},{11,... | collective-permute-start | bytes 4915208 | tf_op jit(solution)/shard_map/ppermute | solution.py:615
  33.4 5.9 %collective-permute-start.7 = (bf16[10240,128]{1,0:T(8,128)(2,1)S(1)}, bf16[10240,128]{1,0:T(8,128)(2,1)S(1)}, u32[]{:S(2)}, u32[]{:S(2)}) collective-permute-start(bf16[10240,128]{1,0:T(8,128)(2,1)S(1)} %get-tuple-element.80), channel_id=1, source_target_pairs={{0,1},{1,0},{2,3},{3,2},{4,5},{5,4},{6,7},{7,6},{8,9},{9,8},{10,11... | collective-permute-start | bytes 7864328 | tf_op jit(solution)/shard_map/ppermute | solution.py:615
  33.5 5.8 %copy-start.9 = (s32[8,4]{0,1:T(4,128)S(1)}, s32[8,4]{0,1:T(4,128)}, u32[]{:S(2)}) copy-start(s32[8,4]{0,1:T(4,128)} %param.16) | copy-start | bytes 388
  33.5 5.8 %copy-start.11 = (f32[8,4]{0,1:T(4,128)S(1)}, f32[8,4]{0,1:T(4,128)}, u32[]{:S(2)}) copy-start(f32[8,4]{0,1:T(4,128)} %param.17) | copy-start | bytes 388
  80.0 7.7 %copy-start.4 = (s32[128,320]{0,1:T(8,128)S(1)}, s32[128,320]{0,1:T(8,128)}, u32[]{:S(2)}) copy-start(s32[128,320]{0,1:T(8,128)} %param.12) | copy-start | bytes 491524
  80.0 7.7 %copy-start.8 = (f32[128,320]{0,1:T(8,128)S(1)}, f32[128,320]{0,1:T(8,128)}, u32[]{:S(2)}) copy-start(f32[128,320]{0,1:T(8,128)} %param.13) | copy-start | bytes 491524
